TPU v7x, 256 devices: a whole 4x4x8 slice. The times are simulated.
256 devices in a mesh: gz: 64 (over z, x, core), gx: 4 (over y).
Axes of the slice: x: 4, y: 4, z: 8, core: 2. Of those that a mesh axis runs over, the one named last changes fastest.
Arguments:
- field: bfloat16 [128, 32, 256, 256], P('gz', None, 'gx'), may hold values from -6 to 6
- spectral_weight: bfloat16 [1024, 2, 32, 1024], P(('gz', 'gx')), may hold values from -1 to 1
- bypass_weight: bfloat16 [32, 32], replicated, may hold values from -1 to 1
- bypass_bias: float32 [32], replicated, may hold values from -1 to 1
Outputs:
- output: bfloat16 [128, 32, 256, 256], P('gz', None, 'gx')
All inputs are finite; a program needn't handle non-finite values.
Results may differ from a plain program's by a relative error of at most 0.0044.
Values may be sent and summed in bfloat16 or wider, within the bound.
A program may use at most 128 MiB of HBM per device.

v0:
```python
import math

import jax
import jax.numpy as jnp
from jax import lax
from jax.sharding import PartitionSpec as P

KX = 32
KY = 32
KZ = 32
NY = 256


def mode_frequencies(modes_count):
    positions = jnp.arange(modes_count, dtype=jnp.int32)
    return jnp.where(positions < modes_count // 2, positions, positions - modes_count)


def phase_table(frequencies, places, length):
    phases = jnp.mod(frequencies[:, None] * places[None, :], length)
    angles = phases.astype(jnp.float32) * (2.0 * math.pi / length)
    return (jnp.cos(angles), jnp.sin(angles))


def pencil_spectrum(block, x_places, length_x):
    block_count, channels, width_x, width_y = block.shape
    cos_y, sin_y = phase_table(mode_frequencies(KY), jnp.arange(width_y, dtype=jnp.int32), width_y)
    table_y = jnp.concatenate([cos_y, -sin_y], axis=0).T.astype(jnp.bfloat16)
    along_y = jnp.dot(block.reshape(-1, width_y), table_y, preferred_element_type=jnp.float32)
    along_y = along_y.reshape(block_count, channels, width_x, 2, KY)
    real_y = along_y[:, :, :, 0]
    imag_y = along_y[:, :, :, 1]
    cos_x, sin_x = phase_table(mode_frequencies(KX), x_places, length_x)
    highest = lax.Precision.HIGHEST
    real_x = jnp.einsum("bcxa,kx->bakc", real_y, cos_x, precision=highest) + jnp.einsum(
        "bcxa,kx->bakc", imag_y, sin_x, precision=highest
    )
    imag_x = jnp.einsum("bcxa,kx->bakc", imag_y, cos_x, precision=highest) - jnp.einsum(
        "bcxa,kx->bakc", real_y, sin_x, precision=highest
    )
    return jnp.stack([real_x, imag_x], axis=0).reshape(2, block_count, KY * KX, channels)


def slab_spectrum(pencils, z_places, length_z):
    cos_z, sin_z = phase_table(jnp.arange(KZ, dtype=jnp.int32), z_places, length_z)
    highest = lax.Precision.HIGHEST
    real_part = jnp.einsum("kb,bqc->kqc", cos_z, pencils[0], precision=highest) + jnp.einsum(
        "kb,bqc->kqc", sin_z, pencils[1], precision=highest
    )
    imag_part = jnp.einsum("kb,bqc->kqc", cos_z, pencils[1], precision=highest) - jnp.einsum(
        "kb,bqc->kqc", sin_z, pencils[0], precision=highest
    )
    return jnp.stack([real_part, imag_part], axis=1)


def mix_modes(spectrum, weight):
    owned_pairs, two_parts, channels, wide = weight.shape
    full_weight = weight.astype(jnp.float32).reshape(owned_pairs, 2, channels, KZ, channels)
    highest = lax.Precision.HIGHEST
    weight_real = full_weight[:, 0]
    weight_imag = full_weight[:, 1]
    spec_real = spectrum[:, 0]
    spec_imag = spectrum[:, 1]
    mixed_real = jnp.einsum(
        "kqi,qiko->kqo", spec_real, weight_real, precision=highest
    ) - jnp.einsum("kqi,qiko->kqo", spec_imag, weight_imag, precision=highest)
    mixed_imag = jnp.einsum(
        "kqi,qiko->kqo", spec_real, weight_imag, precision=highest
    ) + jnp.einsum("kqi,qiko->kqo", spec_imag, weight_real, precision=highest)
    return jnp.stack([mixed_real, mixed_imag], axis=1).astype(jnp.bfloat16)


def plane_values(mixed_modes, z_places, length_z):
    frequencies = jnp.arange(KZ, dtype=jnp.int32)
    factors = jnp.where(frequencies == 0, 1.0, 2.0) / (2.0 * math.sqrt(KX * KY * KZ))
    cos_z, sin_z = phase_table(frequencies, z_places, length_z)
    cos_z = cos_z * factors[:, None]
    sin_z = sin_z * factors[:, None]
    mode_real = mixed_modes[:, 0].astype(jnp.float32)
    mode_imag = mixed_modes[:, 1].astype(jnp.float32)
    highest = lax.Precision.HIGHEST
    real_part = jnp.einsum("kz,kqc->zqc", cos_z, mode_real, precision=highest) - jnp.einsum(
        "kz,kqc->zqc", sin_z, mode_imag, precision=highest
    )
    imag_part = jnp.einsum("kz,kqc->zqc", sin_z, mode_real, precision=highest) + jnp.einsum(
        "kz,kqc->zqc", cos_z, mode_imag, precision=highest
    )
    return jnp.stack([real_part, imag_part], axis=1)


def grid_values(planes, x_places, length_x):
    plane_count = planes.shape[0]
    channels = planes.shape[3]
    shaped = planes.reshape(plane_count, 2, KY, KX, channels)
    cos_x, sin_x = phase_table(mode_frequencies(KX), x_places, length_x)
    highest = lax.Precision.HIGHEST
    real_h = jnp.einsum("zakc,kx->zcxa", shaped[:, 0], cos_x, precision=highest) - jnp.einsum(
        "zakc,kx->zcxa", shaped[:, 1], sin_x, precision=highest
    )
    imag_h = jnp.einsum("zakc,kx->zcxa", shaped[:, 0], sin_x, precision=highest) + jnp.einsum(
        "zakc,kx->zcxa", shaped[:, 1], cos_x, precision=highest
    )
    cos_y, sin_y = phase_table(mode_frequencies(KY), jnp.arange(NY, dtype=jnp.int32), NY)
    table_y = jnp.concatenate([cos_y, -sin_y], axis=0)
    joined = jnp.concatenate([real_h, imag_h], axis=-1)
    width_x = joined.shape[2]
    values = jnp.dot(joined.reshape(-1, 2 * KY), table_y, precision=highest)
    return values.reshape(plane_count, channels, width_x, NY)


def shards(field, spectral_weight, bypass_weight, bypass_bias):
    slab_depth, channels, width_x, width_y = field.shape
    groups_z = lax.axis_size("gz")
    groups_x = lax.axis_size("gx")
    length_z = slab_depth * groups_z
    length_x = width_x * groups_x
    z_places = lax.axis_index("gz") * slab_depth + jnp.arange(slab_depth, dtype=jnp.int32)
    x_places = lax.axis_index("gx") * width_x + jnp.arange(width_x, dtype=jnp.int32)
    forward_scale = 1.0 / math.sqrt(length_x * width_y * length_z)
    owned_pairs = spectral_weight.shape[0]
    pencils = pencil_spectrum(field, x_places, length_x) * forward_scale
    partial_value = slab_spectrum(pencils, z_places, length_z)
    partial_value = partial_value.reshape(KZ, 2, groups_z * groups_x, owned_pairs * channels)
    summed = lax.psum_scatter(partial_value, ("gz", "gx"), scatter_dimension=2, tiled=True)
    spectrum = summed.reshape(KZ, 2, owned_pairs, channels)
    mixed_modes = mix_modes(spectrum, spectral_weight)
    gathered = lax.all_gather(
        mixed_modes.reshape(KZ, 2, 1, owned_pairs * channels), ("gz", "gx"), axis=2, tiled=True
    )
    planes = plane_values(gathered.reshape(KZ, 2, -1, channels), z_places, length_z)
    values = grid_values(planes, x_places, length_x)
    direct = jnp.einsum("zcxy,cd->zdxy", field, bypass_weight, preferred_element_type=jnp.float32)
    total = values + direct + bypass_bias[None, :, None, None]
    return jax.nn.gelu(total, approximate=False).astype(jnp.bfloat16)


def solution(mesh):
    in_specs = (P("gz", None, "gx", None), P(("gz", "gx"), None, None, None), P(), P())
    out_specs = P("gz", None, "gx", None)
    return jax.shard_map(shards, mesh=mesh, in_specs=in_specs, out_specs=out_specs, check_vma=False)
```

profile of v0, /device:TPU:1, one launch (start us, length us, event | category | flops | bytes accessed | tf_op | source)
XLA Modules:
  0.0 1615.7 jit_solution(15664499922872528537)
XLA Ops:
  13.8 5.0 fusion.34
  18.8 7.2 fusion.35
  26.0 5.7 fusion.27
  36.2 6.9 fusion.26
  47.2 3.7 fusion.50
  50.9 5.8 fusion.51
  56.7 5.5 convolution_add_fusion
  62.2 10.6 copy.48
  72.7 12.0 stack.33
  84.7 7.0 convolution_subtract_fusion
  91.7 10.6 copy.49
  102.2 12.0 stack.34
  114.2 4.0 pad_maximum_fusion
  118.3 8.1 copy.50
  130.1 3.1 slice_bitcast_fusion.1
  133.2 1272.0 %reduce-scatter.2.cloned.1.call-done = f32[32,2,1,128]{3,0,1,2:T(8,128)} async-done(((f32[32,2,256,128]{3,0,1,2:T(8,128)}), f32[32,2,1,128]{3,0,1,2:T(8,128)}) %reduce-scatter.2.cloned.1.call-update) | async-done | bytes 32784 | tf_op jit(solution)/shard_map/reduce_scatter | solution.py:124
  1414.2 3.4 fusion.22
  1417.6 107.4 %all-gather.2.cloned.1.call-done = bf16[32,2,256,128]{3,0,2,1:T(8,128)(2,1)} async-done(((bf16[32,2,1,128]{3,0,2,1:T(8,128)(2,1)}), bf16[32,2,256,128]{3,0,2,1:T(8,128)(2,1)}) %all-gather.2.cloned.1.call-update) | async-done | bytes 4194320 | tf_op jit(solution)/shard_map/all_gather | solution.py:127
  1525.0 5.8 copy.51
  1530.8 18.7 %reshape.97 = bf16[32,2,1024,32]{3,2,1,0:T(8,128)(2,1)} reshape(bf16[32,2,256,128]{3,2,1,0:T(8,128)(2,1)} %copy.51) | data formatting | bytes 8388608 | tf_op jit(solution)/shard_map/reshape | solution.py:130
  1549.5 11.5 fusion.180
  1561.0 7.7 copy.83
  1570.8 7.5 copy.82
  1592.7 15.8 fusion.2
  (55 shorter events, 44.9 us)
Async XLA Ops:
  6.5 1.6 copy-start
  6.5 1398.6 %reduce-scatter.2.cloned.1.call-start = ((), (), s32[]{:S(2)}) async-start(), calls=%async_computation.1 | async-start | bytes 8421376 | tf_op jit(solution)/shard_map/reduce_scatter | solution.py:124
  13.8 12.2 copy-start.2
  126.3 1.0 copy-start.5
  126.4 1398.6 %all-gather.2.cloned.1.call-start = ((), (), s32[]{:S(2)}) async-start(), calls=%async_computation.2 | async-start | bytes 4210688 | tf_op jit(solution)/shard_map/all_gather | solution.py:127
  130.1 1284.1 %copy-start.6 = (bf16[32,32]{1,0:T(8,128)(2,1)S(1)}, bf16[32,32]{1,0:T(8,128)(2,1)}, u32[]{:S(2)}) copy-start(bf16[32,32]{1,0:T(8,128)(2,1)} %param.6) | copy-start | bytes 6148
  1585.7 5.8 copy-start.4
  1587.5 5.2 copy-start.7
  1588.9 3.7 copy-start.3
  1592.6 15.8 copy-start.1
Sparse Core Ops, SparseCore 0:
  126.5 1278.6 reduce-scatter.1
  1414.3 110.6 all-gather.1
where the time goes:
time: 1630 us; the launch traced here: 1620 us
  waiting for transfers between devices  1380 us (85%)
  local copies, waits for them, and re-layouts  129 us (8%)
  matrix products  87.3 us (5%)
    reduce_scatter x1, waiting for transfers between devices, shards(): lax.psum_scatter(partial_value, ('gz', 'gx'), scatter_dimension=2, tiled=...  1270 us
    all_gather x1, waiting for transfers between devices, shards(): lax.all_gather(mixed_modes.reshape(KZ, 2, 1, owned_pairs * channels), ('g...  107 us
  transfers between devices with their start and end apart: 2, of which 2 were waited for; matrix products, arithmetic and copies ran while one was open for 1% of the time, Pallas kernels for 0%

commit v1 on v0

v1 whole, which is shorter than its diff:
```python
import math

import jax
import jax.numpy as jnp
import ml_dtypes
import numpy as np
from jax import lax
from jax.experimental import pallas as pl
from jax.experimental.pallas import tpu as pltpu
from jax.sharding import PartitionSpec as P

NX, NY, NZ = 256, 256, 128
BF16 = jnp.bfloat16
F32 = jnp.float32
MESH = pl.DeviceIdType.MESH
NT = (((1,), (1,)), ((), ()))
TN = (((0,), (0,)), ((), ()))


def split(table):
    high = table.astype(ml_dtypes.bfloat16)
    low = (table - high.astype(np.float64)).astype(ml_dtypes.bfloat16)
    return high, low


def wave(frequency, place, length):
    angle = 2.0 * math.pi * np.mod(frequency * place, length) / length
    return np.cos(angle), np.sin(angle)


def signed(mode):
    return np.where(mode < 16, mode, mode - 32)


def axes(*sizes):
    return np.meshgrid(*[np.arange(size) for size in sizes], indexing="ij")


def one_hot(rows, columns, size):
    table = np.zeros((size, size), np.float64)
    table[rows.reshape(-1), columns.reshape(-1)] = 1.0
    return table.astype(ml_dtypes.bfloat16)


def forward_x():
    gx, px, hi, j, c, cc, x = axes(4, 2, 8, 4, 4, 4, 64)
    cos, sin = wave(signed(4 * hi + j), 64 * gx + x, NX)
    table = np.where(px == 0, cos, -sin) * (c == cc)
    return np.stack(split(table.reshape(4, 256, 256)), axis=1)


def forward_y():
    xd, part, zd, px, y = axes(4, 2, 8, 2, NY)
    cos, sin = wave(signed(4 * zd + xd), y, NY)
    table = np.where(px == part, cos, np.where(part == 0, sin, -sin))
    return table.reshape(64, 2 * NY).astype(ml_dtypes.bfloat16)


def order_to_owner():
    xs, b, core, part, zd = axes(4, 2, 2, 2, 8)
    source = (((xs * 2 + b) * 2 + core) * 2 + part) * 8 + zd
    target = (((zd * 2 + core) * 4 + xs) * 2 + b) * 2 + part
    return one_hot(target, source, 256)


def order_to_grid():
    xs, b, core, part, zs = axes(4, 2, 2, 2, 8)
    target = (((xs * 2 + b) * 2 + core) * 2 + part) * 8 + zs
    source = (((zs * 2 + core) * 4 + xs) * 2 + b) * 2 + part
    return one_hot(target, source, 256)


def order_channels():
    j, i = axes(4, 32)
    return one_hot(j * 32 + i, (i // 4) * 16 + j * 4 + i % 4, 128)


def forward_z():
    zs, core, xs, b, part, part_out, kz, o = axes(8, 2, 4, 2, 2, 2, 32, 32)
    cos, sin = wave(kz, 16 * zs + 4 * xs + 2 * core + b, NZ)
    table = np.where(part == part_out, cos, np.where(part_out == 0, sin, -sin)) / math.sqrt(NX * NY * NZ)
    return np.stack(split(table.reshape(256, 2048)))


def turn_lanes():
    table = np.zeros((128, 4, 128), np.float64)
    turn, low, o = axes(4, 4, 32)
    j = (low + turn) % 4
    table[low * 32 + o, turn, (o // 4) * 16 + j * 4 + o % 4] = 1.0
    return table.reshape(128, 512).astype(ml_dtypes.bfloat16)


def inverse_z():
    zd, core, xd, b, part_out, turn, high, part, j = axes(8, 2, 4, 2, 2, 4, 8, 2, 4)
    kz = 4 * high + (j - turn) % 4
    cos, sin = wave(kz, 16 * zd + 4 * xd + 2 * core + b, NZ)
    table = np.where(part == part_out, cos, np.where(part_out == 0, -sin, sin))
    table = table * np.where(kz == 0, 1.0, 2.0) / (2.0 * math.sqrt(32 * 32 * 32))
    return np.stack(split(table.reshape(256, 256)))


def inverse_y():
    xs, part, zs, part_out, y = axes(4, 2, 8, 2, NY)
    cos, sin = wave(signed(4 * zs + xs), y, NY)
    table = np.where(part == part_out, cos, np.where(part_out == 0, -sin, sin))
    return np.concatenate(split(table.reshape(64, 2 * NY)))


def inverse_x():
    gx, group, o, x, part, hi, j, oo = axes(4, 4, 4, 16, 2, 8, 4, 4)
    cos, sin = wave(signed(4 * hi + j), 64 * gx + 16 * group + x, NX)
    table = np.where(part == 0, cos, -sin) * (o == oo)
    return np.concatenate(split(table.reshape(4, 4, 64, 256)), axis=2)


def forward_kernel(field_ref, table_x_ref, table_y_ref, out_ref, field, table_x, along, sems):
    gx = lax.axis_index("gx")
    fetch_x = pltpu.make_async_copy(table_x_ref.at[gx], table_x, sems.at[4])
    fetch_x.start()
    fetches = []
    for part in range(4):
        b, half = part // 2, part % 2
        fetch = pltpu.make_async_copy(
            field_ref.at[b, pl.ds(16 * half, 16)], field.at[part], sems.at[part]
        )
        fetch.start()
        fetches.append(fetch)
    fetch_x.wait()
    for part in range(4):
        b, half = part // 2, part % 2
        fetches[part].wait()
        for inner in range(4):
            group = 4 * half + inner
            block = field[part, 4 * inner : 4 * inner + 4].reshape(256, NY)
            modes = jnp.dot(table_x[0], block, preferred_element_type=F32)
            modes += jnp.dot(table_x[1], block, preferred_element_type=F32)
            modes = modes.astype(BF16)
            for px in range(2):
                for hi in range(8):
                    row = (b * 8 + hi) * 128 + group * 16
                    at = (px * 8 + hi) * 16
                    along[row : row + 16, px * NY : (px + 1) * NY] = modes[at : at + 16]
    for b in range(2):
        for core in range(2):
            row = (b * 2 + core) * 512
            pencil = lax.dot_general(
                table_y_ref[...], along[row : row + 512], NT, preferred_element_type=F32
            ).astype(BF16)
            at = (b * 2 + core) * 16
            for xd in range(4):
                for yd in range(4):
                    out_ref[xd * 4 + yd, at : at + 16, :] = pencil[
                        xd * 16 : xd * 16 + 16, yd * 128 : yd * 128 + 128
                    ]


def exchange_kernel(
    send_ref, weight_ref, to_owner_ref, channels_ref, table_z_ref, turn_ref, back_z_ref, to_grid_ref,
    out_ref,
    got_a, send_b, got_b, back_b, home_b, back_a,
    weight, to_owner, channels, table_z, turn, back_z, to_grid,
    sems, send_sems, recv_sems,
):
    gz = lax.axis_index("gz")
    y = lax.axis_index("gx")
    core = lax.rem(gz, 2)
    x = lax.rem(lax.div(gz, 2), 4)
    z = lax.div(gz, 8)

    def plane_device(index):
        return ((z * 4 + lax.div(index, 4)) * 2 + core, lax.rem(index, 4))

    def line_device(index):
        return ((lax.div(index, 2) * 4 + x) * 2 + lax.rem(index, 2), y)

    plane_me = x * 4 + y
    line_me = z * 2 + core
    arrival = y * 4 + x

    barrier = pltpu.get_barrier_semaphore()

    def greet(step, carry):
        pl.semaphore_signal(
            barrier, inc=1, device_id=plane_device(lax.rem(plane_me + step, 16)), device_id_type=MESH
        )
        pl.semaphore_signal(
            barrier, inc=1, device_id=line_device(lax.rem(line_me + step, 16)), device_id_type=MESH
        )
        return carry

    lax.fori_loop(1, 16, greet, 0)

    fetches = []
    for at, (source, target) in enumerate(
        (
            (to_owner_ref, to_owner), (channels_ref, channels), (table_z_ref, table_z),
            (weight_ref, weight), (turn_ref, turn), (back_z_ref, back_z), (to_grid_ref, to_grid),
        )
    ):
        fetch = pltpu.make_async_copy(source, target, sems.at[at])
        fetch.start()
        fetches.append(fetch)

    got_a[arrival] = send_ref[plane_me]
    pl.semaphore_wait(barrier, 30)

    def plane_copy(phase, index, source, target):
        return pltpu.make_async_remote_copy(
            src_ref=source, dst_ref=target,
            send_sem=send_sems.at[phase, index], recv_sem=recv_sems.at[phase, arrival],
            device_id=plane_device(index), device_id_type=MESH,
        )

    def line_copy(phase, index, source, target):
        return pltpu.make_async_remote_copy(
            src_ref=source, dst_ref=target,
            send_sem=send_sems.at[phase, index], recv_sem=recv_sems.at[phase, line_me],
            device_id=line_device(index), device_id_type=MESH,
        )

    def arrived(phase, index, block):
        pltpu.make_async_copy(block, block, recv_sems.at[phase, index]).wait()

    def each(body):
        lax.fori_loop(1, 16, lambda step, carry: (body(step), carry)[1], 0)

    def send_plane(step):
        index = lax.rem(plane_me + step, 16)
        plane_copy(0, index, send_ref.at[index], got_a.at[arrival]).start()

    each(send_plane)

    def take_plane(step):
        index = lax.rem(arrival + step, 16)
        arrived(0, index, got_a.at[index])

    each(take_plane)
    fetches[0].wait()
    summed = jnp.zeros((256, 128), F32)
    for sy in range(4):
        summed += jnp.dot(
            to_owner[...], got_a[sy * 4 : sy * 4 + 4].reshape(256, 128), preferred_element_type=F32
        )
    send_b[...] = summed.astype(BF16).reshape(16, 16, 128)

    got_b[line_me] = send_b[line_me]

    def send_line(step):
        index = lax.rem(line_me + step, 16)
        line_copy(1, index, send_b.at[index], got_b.at[line_me]).start()

    each(send_line)
    for fetch in fetches[1:]:
        fetch.wait()

    def take_line(step):
        index = lax.rem(line_me + step, 16)
        arrived(1, index, got_b.at[index])

    each(take_line)
    pencils = lax.dot_general(
        channels[...], got_b[...].reshape(256, 128), NT, preferred_element_type=F32
    ).astype(BF16)
    rows = []
    for part in range(2):
        for j in range(4):
            rows.append([])
    for block in range(4):
        real_at, imag_at = block * 256, 1024 + block * 256
        real = jnp.dot(pencils, table_z[0, :, real_at : real_at + 256], preferred_element_type=F32)
        real += jnp.dot(pencils, table_z[1, :, real_at : real_at + 256], preferred_element_type=F32)
        imag = jnp.dot(pencils, table_z[0, :, imag_at : imag_at + 256], preferred_element_type=F32)
        imag += jnp.dot(pencils, table_z[1, :, imag_at : imag_at + 256], preferred_element_type=F32)
        for j in range(4):
            weight_real = weight[j, 0, :, real_at : real_at + 256].astype(F32)
            weight_imag = weight[j, 1, :, real_at : real_at + 256].astype(F32)
            one, two = real[j * 32 : j * 32 + 32], imag[j * 32 : j * 32 + 32]
            rows[j].append(jnp.sum(one * weight_real - two * weight_imag, axis=0, keepdims=True))
            rows[4 + j].append(jnp.sum(one * weight_imag + two * weight_real, axis=0, keepdims=True))
    mixed = jnp.concatenate([jnp.concatenate(row, axis=1) for row in rows], axis=0).astype(BF16)
    mixed = jnp.concatenate([mixed[:, h * 128 : h * 128 + 128].astype(F32) for h in range(8)], axis=0)
    turned = jnp.dot(mixed.astype(BF16), turn[...], preferred_element_type=F32)
    turned = jnp.concatenate([turned[:, t * 128 : t * 128 + 128] for t in range(4)], axis=0)
    row = lax.broadcasted_iota(jnp.int32, (256, 128), 0)
    lane = lax.broadcasted_iota(jnp.int32, (256, 128), 1)
    turned = jnp.where(lax.rem(row, 4) == lax.rem(lax.div(lane, 4), 4), turned, 0.0).astype(BF16)
    planes = jnp.dot(back_z[0], turned, preferred_element_type=F32)
    planes += jnp.dot(back_z[1], turned, preferred_element_type=F32)
    back_b[...] = planes.astype(BF16).reshape(16, 16, 128)

    home_b[line_me] = back_b[line_me]

    def return_line(step):
        index = lax.rem(line_me + step, 16)
        line_copy(2, index, back_b.at[index], home_b.at[line_me]).start()

    each(return_line)

    def home_line(step):
        index = lax.rem(line_me + step, 16)
        arrived(2, index, home_b.at[index])

    each(home_line)
    home = jnp.dot(to_grid[...], home_b[...].reshape(256, 128), preferred_element_type=F32)
    back_a[...] = home.astype(BF16).reshape(4, 64, 128)

    out_ref[arrival] = back_a[x]

    def return_plane(step):
        index = lax.rem(plane_me + step, 16)
        plane_copy(3, index, back_a.at[lax.div(index, 4)], out_ref.at[arrival]).start()

    each(return_plane)

    def home_plane(step):
        index = lax.rem(arrival + step, 16)
        arrived(3, index, out_ref.at[index])

    each(home_plane)

    def sent(step):
        plane_index = lax.rem(plane_me + step, 16)
        line_index = lax.rem(line_me + step, 16)
        plane_copy(0, plane_index, send_ref.at[plane_index], got_a.at[arrival]).wait_send()
        line_copy(1, line_index, send_b.at[line_index], got_b.at[line_me]).wait_send()
        line_copy(2, line_index, back_b.at[line_index], home_b.at[line_me]).wait_send()
        plane_copy(
            3, plane_index, back_a.at[lax.div(plane_index, 4)], out_ref.at[arrival]
        ).wait_send()

    each(sent)


def grid_kernel(
    modes_ref, field_ref, table_y_ref, table_x_ref, bypass_ref, bias_ref, out_ref,
    along, direct_table, bias, table_x, sem,
):
    b, group = pl.program_id(0), pl.program_id(1)

    @pl.when((b == 0) & (group == 0))
    def _():
        gx = lax.axis_index("gx")
        fetch = pltpu.make_async_copy(table_x_ref.at[gx], table_x, sem)
        fetch.start()
        row = lax.div(lax.broadcasted_iota(jnp.int32, (512, 32), 0), 16)
        lane = lax.broadcasted_iota(jnp.int32, (512, 32), 1)
        spread = (row == lane).astype(F32)
        bias[...] = jnp.sum(spread * bias_ref[...], axis=1, keepdims=True)
        spread = spread.astype(BF16)
        wide = lax.dot_general(spread, bypass_ref[...], NT, preferred_element_type=F32).astype(BF16)
        wide = lax.dot_general(wide, spread, NT, preferred_element_type=F32)
        one = lax.rem(lax.broadcasted_iota(jnp.int32, (512, 512), 0), 16)
        two = lax.rem(lax.broadcasted_iota(jnp.int32, (512, 512), 1), 16)
        direct_table[...] = jnp.where(one == two, wide, 0.0).astype(BF16)
        fetch.wait()

    @pl.when(group == 0)
    def _():
        for core in range(2):
            for ys in range(4):
                rows = modes_ref[ys * 4 : ys * 4 + 4, pl.ds(b * 32 + core * 16, 16), :].reshape(64, 128)
                rows = jnp.concatenate([rows, rows], axis=0)
                lines = lax.dot_general(rows, table_y_ref[...], TN, preferred_element_type=F32)
                lines = lines.astype(BF16)
                for part in range(2):
                    at = (part * 8 + core * 4 + ys) * 16
                    for channel in range(8):
                        along[channel, at : at + 16, :] = lines[
                            channel * 16 : channel * 16 + 16, part * NY : (part + 1) * NY
                        ]

    direct = jnp.dot(
        direct_table[...], field_ref[0].reshape(512, NY), preferred_element_type=F32
    )
    for channel in range(8):
        values = jnp.dot(table_x[group], along[channel], preferred_element_type=F32)
        at = channel * 64
        total = values[:64] + values[64:] + direct[at : at + 64] + bias[at : at + 64]
        result = 0.5 * total * (1.0 + lax.erf(total * (1.0 / math.sqrt(2.0))))
        out_ref[0, channel * 4 : channel * 4 + 4] = result.astype(BF16).reshape(4, 16, NY)


VMEM = pl.BlockSpec(memory_space=pltpu.VMEM)
ANY = pl.BlockSpec(memory_space=pl.ANY)


def shards(field, spectral_weight, bypass_weight, bypass_bias):
    pencils = pl.pallas_call(
        forward_kernel,
        out_shape=jax.ShapeDtypeStruct((16, 64, 128), BF16),
        in_specs=[ANY, ANY, VMEM],
        out_specs=VMEM,
        scratch_shapes=[
            pltpu.VMEM((4, 16, 64, NY), BF16),
            pltpu.VMEM((2, 256, 256), BF16),
            pltpu.VMEM((2048, 2 * NY), BF16),
            pltpu.SemaphoreType.DMA((5,)),
        ],
        compiler_params=pltpu.CompilerParams(vmem_limit_bytes=24 << 20),
        name="forward",
    )(field, jnp.asarray(forward_x()), jnp.asarray(forward_y()))

    modes = pl.pallas_call(
        exchange_kernel,
        out_shape=jax.ShapeDtypeStruct((16, 64, 128), BF16),
        in_specs=[VMEM] + [ANY] * 7,
        out_specs=VMEM,
        scratch_shapes=[
            pltpu.VMEM((16, 64, 128), BF16),
            pltpu.VMEM((16, 16, 128), BF16),
            pltpu.VMEM((16, 16, 128), BF16),
            pltpu.VMEM((16, 16, 128), BF16),
            pltpu.VMEM((16, 16, 128), BF16),
            pltpu.VMEM((4, 64, 128), BF16),
            pltpu.VMEM((4, 2, 32, 1024), BF16),
            pltpu.VMEM((256, 256), BF16),
            pltpu.VMEM((128, 128), BF16),
            pltpu.VMEM((2, 256, 2048), BF16),
            pltpu.VMEM((128, 512), BF16),
            pltpu.VMEM((2, 256, 256), BF16),
            pltpu.VMEM((256, 256), BF16),
            pltpu.SemaphoreType.DMA((7,)),
            pltpu.SemaphoreType.DMA((4, 16)),
            pltpu.SemaphoreType.DMA((4, 16)),
        ],
        compiler_params=pltpu.CompilerParams(
            collective_id=0, has_side_effects=True, vmem_limit_bytes=24 << 20
        ),
        name="exchange",
    )(
        pencils, spectral_weight, jnp.asarray(order_to_owner()), jnp.asarray(order_channels()),
        jnp.asarray(forward_z()), jnp.asarray(turn_lanes()), jnp.asarray(inverse_z()),
        jnp.asarray(order_to_grid()),
    )

    block = pl.BlockSpec((1, 32, 16, NY), lambda b, group: (b, 0, group, 0))
    return pl.pallas_call(
        grid_kernel,
        grid=(2, 4),
        out_shape=jax.ShapeDtypeStruct(field.shape, BF16),
        in_specs=[VMEM, block, VMEM, ANY, VMEM, VMEM],
        out_specs=block,
        scratch_shapes=[
            pltpu.VMEM((8, 256, NY), BF16),
            pltpu.VMEM((512, 512), BF16),
            pltpu.VMEM((512, 1), F32),
            pltpu.VMEM((4, 128, 256), BF16),
            pltpu.SemaphoreType.DMA,
        ],
        compiler_params=pltpu.CompilerParams(vmem_limit_bytes=24 << 20),
        name="grid",
    )(
        modes, field, jnp.asarray(inverse_y()), jnp.asarray(inverse_x()), bypass_weight,
        bypass_bias.reshape(1, 32),
    )


def solution(mesh):
    in_specs = (P("gz", None, "gx", None), P(("gz", "gx"), None, None, None), P(), P())
    out_specs = P("gz", None, "gx", None)
    return jax.shard_map(shards, mesh=mesh, in_specs=in_specs, out_specs=out_specs, check_vma=False)
```

time: 1630 us -> 48.7 us (0.03)
  waiting for transfers between devices: 1380 us -> 0 us
  local copies, waits for them, and re-layouts: 129 us -> 3.72 us
  matrix products: 87.3 us -> 0 us
  Pallas kernels: 0 us -> 44.6 us
    reduce_scatter x1 -> x0, waiting for transfers between devices: 1270 us -> none  [shards(): lax.psum_scatter(partial_value, ('gz', 'gx'), scatter_dimension=2, tiled=...]
    all_gather x1 -> x0, waiting for transfers between devices: 107 us -> none  [shards(): lax.all_gather(mixed_modes.reshape(KZ, 2, 1, owned_pairs * channels), ('g...]
    dot_general x23 -> x0, matrix products: 87.3 us -> none  [the longest x1 15.8 us: grid_values(): values = jnp.dot(joined.reshape(-1, 2 * KY), table_y, precision=highest)]
    pallas_call x0 -> x3, Pallas kernels: none -> 44.6 us  [the longest x1 35.4 us: shards(): pl.pallas_call(exchange_kernel, out_shape=jax.ShapeDtypeStruct((16, 64, 1...]
    another operation x9 -> x0, local copies, waits for them, and re-layouts: 39.6 us -> none  [the longest x3 32.1 us: slab_spectrum(): return jnp.stack([real_part, imag_part], axis=1)]
    reshape x4 -> x0, local copies, waits for them, and re-layouts: 24.5 us -> none  [the longest x1 18.7 us: shards(): gathered.reshape(KZ, 2, -1, channels)]
  transfers between devices with their start and end apart: 2 -> 0, of which waited for: 2 -> 0; matrix products, arithmetic and copies ran while one was open for 1% -> 0% of each run, Pallas kernels for 0% -> 0%
where the time goes in v1:
time: 48.7 us; the launch traced here: 48.5 us
  Pallas kernels  44.6 us (92%)
  local copies, waits for them, and re-layouts  3.72 us (8%)
    pallas_call x1, Pallas kernels, shards(): pl.pallas_call(exchange_kernel, out_shape=jax.ShapeDtypeStruct((16, 64, 1...  35.4 us
    pallas_call x1, Pallas kernels, shards(): pl.pallas_call(grid_kernel, grid=(2, 4), out_shape=jax.ShapeDtypeStruct(f...  6.66 us
    unnamed x30, local copies, waits for them, and re-layouts  3.72 us
    pallas_call x1, Pallas kernels, shards(): pl.pallas_call(forward_kernel, out_shape=jax.ShapeDtypeStruct((16, 64, 12...  2.55 us

profile of v1, /device:TPU:1, one launch (start us, length us, event | category | flops | bytes accessed | tf_op | source)
XLA Modules:
  0.0 48.5 jit_solution(10754625915382719273)
XLA Ops:
  0.0 1.6 %copy-done = bf16[2,32,64,256]{3,2,1,0:T(8,128)(2,1)S(1)} copy-done((bf16[2,32,64,256]{3,2,1,0:T(8,128)(2,1)S(1)}, bf16[2,32,64,256]{3,2,1,0:T(8,128)(2,1)}, u32[]{:S(2)}) %copy-start) | copy-done | bytes 2097176
  1.6 1.2 %copy-done.3 = bf16[4,2,256,256]{3,2,1,0:T(8,128)(2,1)S(1)} copy-done((bf16[4,2,256,256]{3,2,1,0:T(8,128)(2,1)S(1)}, bf16[4,2,256,256]{3,2,1,0:T(8,128)(2,1)}, u32[]{:S(2)}) %copy-start.3) | copy-done | bytes 1048600
  2.8 0.8 %copy-done.11 = bf16[64,512]{1,0:T(8,128)(2,1)S(1)} copy-done((bf16[64,512]{1,0:T(8,128)(2,1)S(1)}, bf16[64,512]{1,0:T(8,128)(2,1)}, u32[]{:S(2)}) %copy-start.11) | copy-done | bytes 65560
  3.7 0.0 copy-start.9
  3.7 0.0 copy-start.10
  3.7 0.0 copy-start.12
  3.7 2.6 %forward.1.send_ref = bf16[16,64,128]{2,1,0:T(8,128)(2,1)S(1)} custom-call(bf16[2,32,64,256]{3,2,1,0:T(8,128)(2,1)S(1)} %copy-done, bf16[4,2,256,256]{3,2,1,0:T(8,128)(2,1)S(1)} %copy-done.3, bf16[64,512]{1,0:T(8,128)(2,1)S(1)} %copy-done.11), custom_call_target="tpu_custom_call" | custom-call | tf_op jit(solution)/shard_map/forward/pallas_call | solution.py:388
  6.3 0.0 copy-done.2
  6.3 0.0 copy-done.5
  6.3 0.0 copy-done.6
  6.3 0.0 copy-done.8
  6.3 0.0 copy-done.9
  6.3 0.0 copy-start.1
  6.3 0.0 copy-start.4
  6.4 0.0 copy-start.7
  6.4 0.0 copy-start.13
  6.4 0.0 copy-start.14
  6.4 35.4 %exchange.1.modes_ref = bf16[16,64,128]{2,1,0:T(8,128)(2,1)S(1)} custom-call(bf16[16,64,128]{2,1,0:T(8,128)(2,1)S(1)} %forward.1.send_ref, bf16[4,2,32,1024]{3,2,1,0:T(8,128)(2,1)S(1)} %copy-done.5, bf16[256,256]{1,0:T(8,128)(2,1)S(1)} %copy-done.10, bf16[128,128]{1,0:T(8,128)(2,1)S(1)} %copy-done.12, bf16[2,256,2048]{2,1,0:T(8,128)(2,1)S(1)} %copy-done.2, ...), custom_call_target="tpu_custom_call" | custom-call | tf_op jit(solution)/shard_map/exchange/pallas_call | solution.py:403
  41.8 0.0 copy-done.1
  41.8 0.0 copy-done.4
  41.8 0.0 copy-done.7
  41.8 0.0 copy-done.13
  41.8 0.0 copy-done.14
  41.8 6.7 %grid.1 = bf16[2,32,64,256]{3,2,1,0:T(8,128)(2,1)} custom-call(bf16[16,64,128]{2,1,0:T(8,128)(2,1)S(1)} %exchange.1.modes_ref, bf16[2,32,64,256]{3,2,1,0:T(8,128)(2,1)S(1)} %copy-done.1, bf16[128,512]{1,0:T(8,128)(2,1)S(1)} %copy-done.7, bf16[4,4,128,256]{3,2,1,0:T(8,128)(2,1)S(1)} %copy-done.4, bf16[32,32]{1,0:T(8,128)(2,1)S(1)} %copy-done.13, ...), custom_call_target="tpu_custom_call" | custom-call | tf_op jit(solution)/shard_map/grid/pallas_call | solution.py:437
  (9 shorter events, 0.0 us)
Async XLA Ops:
  0.0 1.6 %copy-start = (bf16[2,32,64,256]{3,2,1,0:T(8,128)(2,1)S(1)}, bf16[2,32,64,256]{3,2,1,0:T(8,128)(2,1)}, u32[]{:S(2)}) copy-start(bf16[2,32,64,256]{3,2,1,0:T(8,128)(2,1)} %field_ref.3) | copy-start | bytes 6291460
  1.6 1.2 %copy-start.3 = (bf16[4,2,256,256]{3,2,1,0:T(8,128)(2,1)S(1)}, bf16[4,2,256,256]{3,2,1,0:T(8,128)(2,1)}, u32[]{:S(2)}) copy-start(bf16[4,2,256,256]{3,2,1,0:T(8,128)(2,1)} %constant.20.clone.table_x_ref) | copy-start | bytes 3145732
  2.8 0.8 %copy-start.11 = (bf16[64,512]{1,0:T(8,128)(2,1)S(1)}, bf16[64,512]{1,0:T(8,128)(2,1)}, u32[]{:S(2)}) copy-start(bf16[64,512]{1,0:T(8,128)(2,1)} %constant.21.clone.table_y_ref) | copy-start | bytes 196612
  3.7 2.6 %copy-start.2 = (bf16[2,256,2048]{2,1,0:T(8,128)(2,1)S(1)}, bf16[2,256,2048]{2,1,0:T(8,128)(2,1)}, u32[]{:S(2)}) copy-start(bf16[2,256,2048]{2,1,0:T(8,128)(2,1)} %constant.24.clone.table_z_ref) | copy-start | bytes 6291460
  3.7 2.6 %copy-start.5 = (bf16[4,2,32,1024]{3,2,1,0:T(8,128)(2,1)S(1)}, bf16[4,2,32,1024]{3,2,1,0:T(8,128)(2,1)}, u32[]{:S(2)}) copy-start(bf16[4,2,32,1024]{3,2,1,0:T(8,128)(2,1)} %weight_ref.1) | copy-start | bytes 1572868
  3.7 2.6 %copy-start.6 = (bf16[2,256,256]{2,1,0:T(8,128)(2,1)S(1)}, bf16[2,256,256]{2,1,0:T(8,128)(2,1)}, u32[]{:S(2)}) copy-start(bf16[2,256,256]{2,1,0:T(8,128)(2,1)} %constant.26.clone.back_z_ref) | copy-start | bytes 786436
  3.7 2.6 %copy-start.8 = (bf16[256,256]{1,0:T(8,128)(2,1)S(1)}, bf16[256,256]{1,0:T(8,128)(2,1)}, u32[]{:S(2)}) copy-start(bf16[256,256]{1,0:T(8,128)(2,1)} %constant.27.clone.to_grid_ref) | copy-start | bytes 393220
  3.7 2.6 %copy-start.9 = (bf16[128,512]{1,0:T(8,128)(2,1)S(1)}, bf16[128,512]{1,0:T(8,128)(2,1)}, u32[]{:S(2)}) copy-start(bf16[128,512]{1,0:T(8,128)(2,1)} %constant.25.clone.turn_ref) | copy-start | bytes 393220
  3.7 2.6 %copy-start.10 = (bf16[256,256]{1,0:T(8,128)(2,1)S(1)}, bf16[256,256]{1,0:T(8,128)(2,1)}, u32[]{:S(2)}) copy-start(bf16[256,256]{1,0:T(8,128)(2,1)} %constant.22.clone.to_owner_ref) | copy-start | bytes 393220
  3.7 2.6 %copy-start.12 = (bf16[128,128]{1,0:T(8,128)(2,1)S(1)}, bf16[128,128]{1,0:T(8,128)(2,1)}, u32[]{:S(2)}) copy-start(bf16[128,128]{1,0:T(8,128)(2,1)} %constant.23.clone.channels_ref) | copy-start | bytes 98308
  6.3 35.4 %copy-start.1 = (bf16[2,32,64,256]{3,2,1,0:T(8,128)(2,1)S(1)}, bf16[2,32,64,256]{3,2,1,0:T(8,128)(2,1)}, u32[]{:S(2)}) copy-start(bf16[2,32,64,256]{3,2,1,0:T(8,128)(2,1)} %field_ref.3) | copy-start | bytes 6291460
  6.3 35.4 %copy-start.4 = (bf16[4,4,128,256]{3,2,1,0:T(8,128)(2,1)S(1)}, bf16[4,4,128,256]{3,2,1,0:T(8,128)(2,1)}, u32[]{:S(2)}) copy-start(bf16[4,4,128,256]{3,2,1,0:T(8,128)(2,1)} %constant.29.clone.table_x_ref) | copy-start | bytes 3145732
  6.4 35.4 %copy-start.7 = (bf16[128,512]{1,0:T(8,128)(2,1)S(1)}, bf16[128,512]{1,0:T(8,128)(2,1)}, u32[]{:S(2)}) copy-start(bf16[128,512]{1,0:T(8,128)(2,1)} %constant.28.clone.table_y_ref) | copy-start | bytes 393220
  6.4 35.4 %copy-start.13 = (bf16[32,32]{1,0:T(8,128)(2,1)S(1)}, bf16[32,32]{1,0:T(8,128)(2,1)}, u32[]{:S(2)}) copy-start(bf16[32,32]{1,0:T(8,128)(2,1)} %bypass_ref.1) | copy-start | bytes 6148
  6.4 35.4 %copy-start.14 = (f32[32]{0:T(128)S(1)}, f32[32]{0:T(128)}, u32[]{:S(2)}) copy-start(f32[32]{0:T(128)} %param.17) | copy-start | bytes 388

commit v2 on v1

v2 whole, which is shorter than its diff:
```python
import math

import jax
import jax.numpy as jnp
import ml_dtypes
import numpy as np
from jax import lax
from jax.experimental import pallas as pl
from jax.experimental.pallas import tpu as pltpu
from jax.sharding import PartitionSpec as P

NX, NY, NZ = 256, 256, 128
BF16 = jnp.bfloat16
F32 = jnp.float32
MESH = pl.DeviceIdType.MESH
NT = (((1,), (1,)), ((), ()))
TN = (((0,), (0,)), ((), ()))


PLANE = [(dx, dy) for dx in range(4) for dy in range(4) if dx or dy]
LINE = [(dz, dc) for dz in range(8) for dc in range(2) if dz or dc]


def ring(step, size):
    return min(step, size - step)


def split(table):
    high = table.astype(ml_dtypes.bfloat16)
    low = (table - high.astype(np.float64)).astype(ml_dtypes.bfloat16)
    return high, low


def wave(frequency, place, length):
    angle = 2.0 * math.pi * np.mod(frequency * place, length) / length
    return np.cos(angle), np.sin(angle)


def signed(mode):
    return np.where(mode < 16, mode, mode - 32)


def axes(*sizes):
    return np.meshgrid(*[np.arange(size) for size in sizes], indexing="ij")


def one_hot(rows, columns, size):
    table = np.zeros((size, size), np.float64)
    table[rows.reshape(-1), columns.reshape(-1)] = 1.0
    return table.astype(ml_dtypes.bfloat16)


def forward_x():
    gx, px, hi, j, c, cc, x = axes(4, 2, 8, 4, 4, 4, 64)
    cos, sin = wave(signed(4 * hi + j), 64 * gx + x, NX)
    table = np.where(px == 0, cos, -sin) * (c == cc)
    return np.stack(split(table.reshape(4, 256, 256)), axis=1)


def forward_y():
    xd, part, zd, px, y = axes(4, 2, 8, 2, NY)
    cos, sin = wave(signed(4 * zd + xd), y, NY)
    table = np.where(px == part, cos, np.where(part == 0, sin, -sin))
    return table.reshape(64, 2 * NY).astype(ml_dtypes.bfloat16)


def order_to_owner():
    xs, b, core, part, zd = axes(4, 2, 2, 2, 8)
    source = (((xs * 2 + b) * 2 + core) * 2 + part) * 8 + zd
    target = (((zd * 2 + core) * 4 + xs) * 2 + b) * 2 + part
    return one_hot(target, source, 256)


def order_to_grid():
    xs, b, core, part, zs = axes(4, 2, 2, 2, 8)
    target = (((xs * 2 + b) * 2 + core) * 2 + part) * 8 + zs
    source = (((zs * 2 + core) * 4 + xs) * 2 + b) * 2 + part
    return one_hot(target, source, 256)


def order_channels():
    j, i = axes(4, 32)
    return one_hot(j * 32 + i, (i // 4) * 16 + j * 4 + i % 4, 128)


def forward_z():
    zs, core, xs, b, part, part_out, kz, o = axes(8, 2, 4, 2, 2, 2, 32, 32)
    cos, sin = wave(kz, 16 * zs + 4 * xs + 2 * core + b, NZ)
    table = np.where(part == part_out, cos, np.where(part_out == 0, sin, -sin)) / math.sqrt(NX * NY * NZ)
    return np.stack(split(table.reshape(256, 2048)))


def turn_lanes():
    table = np.zeros((128, 4, 128), np.float64)
    turn, low, o = axes(4, 4, 32)
    j = (low + turn) % 4
    table[low * 32 + o, turn, (o // 4) * 16 + j * 4 + o % 4] = 1.0
    return table.reshape(128, 512).astype(ml_dtypes.bfloat16)


def inverse_z():
    zd, core, xd, b, part_out, turn, high, part, j = axes(8, 2, 4, 2, 2, 4, 8, 2, 4)
    kz = 4 * high + (j - turn) % 4
    cos, sin = wave(kz, 16 * zd + 4 * xd + 2 * core + b, NZ)
    table = np.where(part == part_out, cos, np.where(part_out == 0, -sin, sin))
    table = table * np.where(kz == 0, 1.0, 2.0) / (2.0 * math.sqrt(32 * 32 * 32))
    return np.stack(split(table.reshape(256, 256)))


def inverse_y():
    xs, part, zs, part_out, y = axes(4, 2, 8, 2, NY)
    cos, sin = wave(signed(4 * zs + xs), y, NY)
    table = np.where(part == part_out, cos, np.where(part_out == 0, -sin, sin))
    return np.concatenate(split(table.reshape(64, 2 * NY)))


def inverse_x():
    gx, o, x, part, hi, j, oo = axes(4, 4, 64, 2, 8, 4, 4)
    cos, sin = wave(signed(4 * hi + j), 64 * gx + x, NX)
    table = np.where(part == 0, cos, -sin) * (o == oo)
    return np.concatenate(split(table.reshape(4, 256, 256)), axis=1)


def exchange_kernel(
    field_ref, table_x_ref, table_y_ref, weight_ref, to_owner_ref, channels_ref, table_z_ref, turn_ref,
    back_z_ref, to_grid_ref, back_y_ref, back_x_ref, bypass_ref, bias_ref,
    out_ref,
    send_a, got_a, send_b, got_b, back_b, home_b, back_a, home_a,
    field, table_x, table_y, along, weight, to_owner, channels, table_z, turn, back_z, to_grid,
    back_y, back_x, direct_table, direct, lines, result,
    sems, send_sems, recv_sems, store_sems,
):
    gz = lax.axis_index("gz")
    y = lax.axis_index("gx")
    core = gz & 1
    x = lax.shift_right_logical(gz, 1) & 3
    z = lax.shift_right_logical(gz, 3)
    xs = [(x + step) & 3 for step in range(4)]
    ys = [(y + step) & 3 for step in range(4)]
    zs = [(z + step) & 7 for step in range(8)]
    cores = [core, 1 - core]

    plane = []
    for dx, dy in sorted(PLANE, key=lambda step: -ring(step[0], 4) - ring(step[1], 4)):
        plane.append((xs[dx] * 4 + ys[dy], ys[dy] * 4 + xs[dx], (z * 8 + xs[dx] * 2 + core, ys[dy])))
    line = []
    for dz, dc in sorted(LINE, key=lambda step: -ring(step[0], 8) - 0.1 * step[1]):
        line.append((zs[dz] * 2 + cores[dc], (zs[dz] * 8 + x * 2 + cores[dc], y)))

    plane_me = x * 4 + y
    line_me = z * 2 + core
    arrival = y * 4 + x

    def fetch(at, source, target):
        copy = pltpu.make_async_copy(source, target, sems.at[at])
        copy.start()
        return copy

    fetch_x = fetch(0, table_x_ref.at[y], table_x)
    fetch_field = []
    for part in range(4):
        source = field_ref.at[part // 2, pl.ds(16 * (part % 2), 16)]
        fetch_field.append(fetch(1 + part, source, field.at[part // 2, pl.ds(16 * (part % 2), 16)]))
    fetch_y = fetch(5, table_y_ref, table_y)

    barrier = pltpu.get_barrier_semaphore()
    for _, device in line:
        pl.semaphore_signal(barrier, inc=1, device_id=device, device_id_type=MESH)
    for _, _, device in plane:
        pl.semaphore_signal(barrier, inc=1, device_id=device, device_id_type=MESH)

    fetch_owner = fetch(6, to_owner_ref, to_owner)
    fetch_center = [
        fetch(7, channels_ref, channels), fetch(8, table_z_ref, table_z), fetch(9, weight_ref, weight),
        fetch(10, turn_ref, turn), fetch(11, back_z_ref, back_z), fetch(12, to_grid_ref, to_grid),
        fetch(13, back_y_ref, back_y), fetch(14, back_x_ref.at[y], back_x),
    ]

    fetch_x.wait()
    for part in range(4):
        b, half = part // 2, part % 2
        fetch_field[part].wait()
        for inner in range(4):
            group = 4 * half + inner
            block = field[b, 4 * group : 4 * group + 4].reshape(256, NY)
            modes = jnp.dot(table_x[0], block, preferred_element_type=F32)
            modes += jnp.dot(table_x[1], block, preferred_element_type=F32)
            modes = modes.astype(BF16)
            for px in range(2):
                for hi in range(8):
                    row = (b * 8 + hi) * 128 + group * 16
                    at = (px * 8 + hi) * 16
                    along[row : row + 16, px * NY : (px + 1) * NY] = modes[at : at + 16]
    fetch_y.wait()
    for b in range(2):
        for half in range(2):
            row = (b * 2 + half) * 512
            pencil = lax.dot_general(
                table_y[...], along[row : row + 512], NT, preferred_element_type=F32
            ).astype(BF16)
            at = (b * 2 + half) * 16
            for xd in range(4):
                for yd in range(4):
                    send_a[xd * 4 + yd, at : at + 16, :] = pencil[
                        xd * 16 : xd * 16 + 16, yd * 128 : yd * 128 + 128
                    ]
    pl.semaphore_wait(barrier, 30)

    sent = []

    def send_plane(phase, source, target):
        for index, _, device in plane:
            copy = pltpu.make_async_remote_copy(
                src_ref=source(index), dst_ref=target.at[arrival],
                send_sem=send_sems.at[phase, index], recv_sem=recv_sems.at[phase, arrival],
                device_id=device, device_id_type=MESH,
            )
            copy.start()
            sent.append(copy)

    def send_line(phase, source, target):
        for index, device in line:
            copy = pltpu.make_async_remote_copy(
                src_ref=source.at[index], dst_ref=target.at[line_me],
                send_sem=send_sems.at[phase, index], recv_sem=recv_sems.at[phase, line_me],
                device_id=device, device_id_type=MESH,
            )
            copy.start()
            sent.append(copy)

    def arrived(phase, index, block):
        pltpu.make_async_copy(block, block, recv_sems.at[phase, index]).wait()

    send_plane(0, lambda index: send_a.at[index], got_a)
    got_a[arrival] = send_a[plane_me]

    row = lax.div(lax.broadcasted_iota(jnp.int32, (512, 32), 0), 16)
    lane = lax.broadcasted_iota(jnp.int32, (512, 32), 1)
    spread = (row == lane).astype(F32)
    bias = jnp.sum(spread * bias_ref[...], axis=1, keepdims=True)
    spread = spread.astype(BF16)
    wide = lax.dot_general(spread, bypass_ref[...], NT, preferred_element_type=F32).astype(BF16)
    wide = lax.dot_general(wide, spread, NT, preferred_element_type=F32)
    one = lax.rem(lax.broadcasted_iota(jnp.int32, (512, 512), 0), 16)
    two = lax.rem(lax.broadcasted_iota(jnp.int32, (512, 512), 1), 16)
    direct_table[...] = jnp.where(one == two, wide, 0.0).astype(BF16)

    def bypass(b):
        for group in range(4):
            block = field[b, :, group * 16 : group * 16 + 16, :].reshape(512, NY)
            values = bias + jnp.dot(direct_table[...], block, preferred_element_type=F32)
            direct[b, :, group * 16 : group * 16 + 16, :] = values.reshape(32, 16, NY)

    bypass(0)

    for _, slot, _ in plane:
        arrived(0, slot, got_a.at[slot])
    fetch_owner.wait()
    summed = jnp.zeros((256, 128), F32)
    for sy in range(4):
        summed += jnp.dot(
            to_owner[...], got_a[sy * 4 : sy * 4 + 4].reshape(256, 128), preferred_element_type=F32
        )
    send_b[...] = summed.astype(BF16).reshape(16, 16, 128)

    send_line(1, send_b, got_b)
    got_b[line_me] = send_b[line_me]
    bypass(1)
    for copy in fetch_center:
        copy.wait()

    for index, _ in line:
        arrived(1, index, got_b.at[index])
    pencils = lax.dot_general(
        channels[...], got_b[...].reshape(256, 128), NT, preferred_element_type=F32
    ).astype(BF16)
    rows = []
    for part in range(2):
        for j in range(4):
            rows.append([])
    for block in range(4):
        real_at, imag_at = block * 256, 1024 + block * 256
        real = jnp.dot(pencils, table_z[0, :, real_at : real_at + 256], preferred_element_type=F32)
        real += jnp.dot(pencils, table_z[1, :, real_at : real_at + 256], preferred_element_type=F32)
        imag = jnp.dot(pencils, table_z[0, :, imag_at : imag_at + 256], preferred_element_type=F32)
        imag += jnp.dot(pencils, table_z[1, :, imag_at : imag_at + 256], preferred_element_type=F32)
        for j in range(4):
            weight_real = weight[j, 0, :, real_at : real_at + 256].astype(F32)
            weight_imag = weight[j, 1, :, real_at : real_at + 256].astype(F32)
            one, two = real[j * 32 : j * 32 + 32], imag[j * 32 : j * 32 + 32]
            rows[j].append(jnp.sum(one * weight_real - two * weight_imag, axis=0, keepdims=True))
            rows[4 + j].append(jnp.sum(one * weight_imag + two * weight_real, axis=0, keepdims=True))
    mixed = jnp.concatenate([jnp.concatenate(row, axis=1) for row in rows], axis=0)
    mixed = jnp.concatenate([mixed[:, h * 128 : h * 128 + 128] for h in range(8)], axis=0)
    turned = jnp.dot(mixed.astype(BF16), turn[...], preferred_element_type=F32)
    turned = jnp.concatenate([turned[:, t * 128 : t * 128 + 128] for t in range(4)], axis=0)
    row = lax.broadcasted_iota(jnp.int32, (256, 128), 0)
    lane = lax.broadcasted_iota(jnp.int32, (256, 128), 1)
    turned = jnp.where(lax.rem(row, 4) == lax.rem(lax.div(lane, 4), 4), turned, 0.0).astype(BF16)
    planes = jnp.dot(back_z[0], turned, preferred_element_type=F32)
    planes += jnp.dot(back_z[1], turned, preferred_element_type=F32)
    back_b[...] = planes.astype(BF16).reshape(16, 16, 128)

    send_line(2, back_b, home_b)
    home_b[line_me] = back_b[line_me]

    for index, _ in line:
        arrived(2, index, home_b.at[index])
    home = jnp.dot(to_grid[...], home_b[...].reshape(256, 128), preferred_element_type=F32)
    back_a[...] = home.astype(BF16).reshape(4, 64, 128)

    send_plane(3, lambda index: back_a.at[lax.shift_right_logical(index, 2)], home_a)
    home_a[arrival] = back_a[x]

    for dy in (0, 1, 3, 2):
        for dx in range(4):
            if dx or dy:
                slot = ys[dy] * 4 + xs[dx]
                arrived(3, slot, home_a.at[slot])
        rows = jnp.concatenate(
            [home_a[pl.ds(ys[dy] * 4, 4), at : at + 16, :].reshape(64, 128) for at in range(0, 64, 16)], axis=1
        )
        rows = jnp.concatenate([rows, rows], axis=0)
        values = lax.dot_general(rows, back_y[...], TN, preferred_element_type=F32).astype(BF16)
        for b in range(2):
            for half in range(2):
                for part in range(2):
                    at = pl.multiple_of((part * 8 + half * 4 + ys[dy]) * 16, 16)
                    for group in range(8):
                        row = (b * 2 + half) * 128 + group * 16
                        lines[b, group, pl.ds(at, 16), :] = values[
                            row : row + 16, part * NY : (part + 1) * NY
                        ]

    def store(b, group):
        rows = pl.ds(group * 4, 4)
        return pltpu.make_async_copy(result.at[b, rows], out_ref.at[b, rows], store_sems.at[b, group])

    def finish(group, carry):
        for b in range(2):
            values = jnp.dot(back_x[...], lines[b, group], preferred_element_type=F32)
            rows = pl.ds(group * 4, 4)
            total = values[:256] + values[256:] + direct[b, rows].reshape(256, NY)
            total = 0.5 * total * (1.0 + lax.erf(total * (1.0 / math.sqrt(2.0))))
            result[b, rows] = total.astype(BF16).reshape(4, 64, NY)
            store(b, group).start()
        return carry

    lax.fori_loop(0, 8, finish, 0)
    for copy in sent:
        copy.wait_send()

    def stored(group, carry):
        for b in range(2):
            store(b, group).wait()
        return carry

    lax.fori_loop(0, 8, stored, 0)


VMEM = pl.BlockSpec(memory_space=pltpu.VMEM)
HBM = pl.BlockSpec(memory_space=pltpu.HBM)


def shards(field, spectral_weight, bypass_weight, bypass_bias):
    return pl.pallas_call(
        exchange_kernel,
        out_shape=jax.ShapeDtypeStruct(field.shape, BF16),
        in_specs=[HBM] * 12 + [VMEM] * 2,
        out_specs=HBM,
        scratch_shapes=[
            pltpu.VMEM((16, 64, 128), BF16),
            pltpu.VMEM((16, 64, 128), BF16),
            pltpu.VMEM((16, 16, 128), BF16),
            pltpu.VMEM((16, 16, 128), BF16),
            pltpu.VMEM((16, 16, 128), BF16),
            pltpu.VMEM((16, 16, 128), BF16),
            pltpu.VMEM((4, 64, 128), BF16),
            pltpu.VMEM((16, 64, 128), BF16),
            pltpu.VMEM((2, 32, 64, NY), BF16),
            pltpu.VMEM((2, 256, 256), BF16),
            pltpu.VMEM((64, 2 * NY), BF16),
            pltpu.VMEM((2048, 2 * NY), BF16),
            pltpu.VMEM((4, 2, 32, 1024), BF16),
            pltpu.VMEM((256, 256), BF16),
            pltpu.VMEM((128, 128), BF16),
            pltpu.VMEM((2, 256, 2048), BF16),
            pltpu.VMEM((128, 512), BF16),
            pltpu.VMEM((2, 256, 256), BF16),
            pltpu.VMEM((256, 256), BF16),
            pltpu.VMEM((128, 512), BF16),
            pltpu.VMEM((512, 256), BF16),
            pltpu.VMEM((512, 512), BF16),
            pltpu.VMEM((2, 32, 64, NY), F32),
            pltpu.VMEM((2, 8, 256, NY), BF16),
            pltpu.VMEM((2, 32, 64, NY), BF16),
            pltpu.SemaphoreType.DMA((15,)),
            pltpu.SemaphoreType.DMA((4, 16)),
            pltpu.SemaphoreType.DMA((4, 16)),
            pltpu.SemaphoreType.DMA((2, 8)),
        ],
        compiler_params=pltpu.CompilerParams(
            collective_id=0, has_side_effects=True, vmem_limit_bytes=60 << 20
        ),
        name="exchange",
    )(
        field, jnp.asarray(forward_x()), jnp.asarray(forward_y()),
        spectral_weight, jnp.asarray(order_to_owner()), jnp.asarray(order_channels()),
        jnp.asarray(forward_z()), jnp.asarray(turn_lanes()), jnp.asarray(inverse_z()),
        jnp.asarray(order_to_grid()), jnp.asarray(inverse_y()), jnp.asarray(inverse_x()),
        bypass_weight, bypass_bias.reshape(1, 32),
    )


def solution(mesh):
    in_specs = (P("gz", None, "gx", None), P(("gz", "gx"), None, None, None), P(), P())
    out_specs = P("gz", None, "gx", None)
    return jax.shard_map(shards, mesh=mesh, in_specs=in_specs, out_specs=out_specs, check_vma=False)
```

time: 48.7 us -> 41.6 us (0.85)
  Pallas kernels: 44.6 us -> 38.2 us
  local copies, waits for them, and re-layouts: 3.72 us -> 3.16 us
    pallas_call x3 -> x1, Pallas kernels: 44.6 us -> 38.2 us  [shards(): pl.pallas_call(exchange_kernel, out_shape=jax.ShapeDtypeStruct(field.shap...]
    unnamed x30 -> x1, local copies, waits for them, and re-layouts: 3.72 us -> 3.16 us
where the time goes in v2:
time: 41.6 us; the launch traced here: 41.4 us
  Pallas kernels  38.2 us (92%)
  local copies, waits for them, and re-layouts  3.16 us (8%)
    pallas_call x1, Pallas kernels, shards(): pl.pallas_call(exchange_kernel, out_shape=jax.ShapeDtypeStruct(field.shap...  38.2 us
    unnamed x1, local copies, waits for them, and re-layouts  3.16 us

profile of v2, /device:TPU:1, one launch (start us, length us, event | category | flops | bytes accessed | tf_op | source)
XLA Modules:
  0.0 41.4 jit_solution(16268124635567818722)
XLA Ops:
  0.0 38.2 %exchange.1 = bf16[2,32,64,256]{3,2,1,0:T(8,128)(2,1)} custom-call(bf16[2,32,64,256]{3,2,1,0:T(8,128)(2,1)} %field_ref.1, bf16[4,2,256,256]{3,2,1,0:T(8,128)(2,1)} %constant.20.clone.table_x_ref, bf16[64,512]{1,0:T(8,128)(2,1)} %constant.21.clone.table_y_ref, bf16[4,2,32,1024]{3,2,1,0:T(8,128)(2,1)} %weight_ref.1, ...), custom_call_target="tpu_custom_call" | custom-call | tf_op jit(solution)/shard_map/exchange/pallas_call | solution.py:366
  38.3 3.2 %copy.16 = bf16[2,32,64,256]{3,2,1,0:T(8,128)(2,1)} copy(bf16[2,32,64,256]{3,2,1,0:T(8,128)(2,1)} %exchange.1) | data formatting | bytes 4194304

commit v3 on v2

--- a/solution.py
+++ b/solution.py
@@ -17,12 +17,16 @@
 TN = (((0,), (0,)), ((), ()))
 
 
-PLANE = [(dx, dy) for dx in range(4) for dy in range(4) if dx or dy]
-LINE = [(dz, dc) for dz in range(8) for dc in range(2) if dz or dc]
-
-
 def ring(step, size):
     return min(step, size - step)
+
+
+PLANE = sorted(
+    [(dx, dy) for dx in range(4) for dy in range(4) if dx or dy], key=lambda step: -ring(step[0], 4) - ring(step[1], 4)
+)
+LINE = sorted(
+    [(dz, dc) for dz in range(8) for dc in range(2) if dz or dc], key=lambda step: -ring(step[0], 8) - 0.1 * step[1]
+)
 
 
 def split(table):
@@ -141,15 +145,24 @@
     cores = [core, 1 - core]
 
     plane = []
-    for dx, dy in sorted(PLANE, key=lambda step: -ring(step[0], 4) - ring(step[1], 4)):
+    for dx, dy in PLANE:
         plane.append((xs[dx] * 4 + ys[dy], ys[dy] * 4 + xs[dx], (z * 8 + xs[dx] * 2 + core, ys[dy])))
     line = []
-    for dz, dc in sorted(LINE, key=lambda step: -ring(step[0], 8) - 0.1 * step[1]):
+    for dz, dc in LINE:
         line.append((zs[dz] * 2 + cores[dc], (zs[dz] * 8 + x * 2 + cores[dc], y)))
 
     plane_me = x * 4 + y
     line_me = z * 2 + core
     arrival = y * 4 + x
+
+    barrier = pltpu.get_barrier_semaphore()
+    for near in range(4, -1, -1):
+        for (dz, _), (_, device) in zip(LINE, line):
+            if ring(dz, 8) == near:
+                pl.semaphore_signal(barrier, inc=1, device_id=device, device_id_type=MESH)
+        for (dx, dy), (_, _, device) in zip(PLANE, plane):
+            if ring(dx, 4) + ring(dy, 4) == near:
+                pl.semaphore_signal(barrier, inc=1, device_id=device, device_id_type=MESH)
 
     def fetch(at, source, target):
         copy = pltpu.make_async_copy(source, target, sems.at[at])
@@ -162,12 +175,6 @@
         source = field_ref.at[part // 2, pl.ds(16 * (part % 2), 16)]
         fetch_field.append(fetch(1 + part, source, field.at[part // 2, pl.ds(16 * (part % 2), 16)]))
     fetch_y = fetch(5, table_y_ref, table_y)
-
-    barrier = pltpu.get_barrier_semaphore()
-    for _, device in line:
-        pl.semaphore_signal(barrier, inc=1, device_id=device, device_id_type=MESH)
-    for _, _, device in plane:
-        pl.semaphore_signal(barrier, inc=1, device_id=device, device_id_type=MESH)
 
     fetch_owner = fetch(6, to_owner_ref, to_owner)
     fetch_center = [
@@ -312,41 +319,40 @@
     send_plane(3, lambda index: back_a.at[lax.shift_right_logical(index, 2)], home_a)
     home_a[arrival] = back_a[x]
 
-    for dy in (0, 1, 3, 2):
-        for dx in range(4):
-            if dx or dy:
-                slot = ys[dy] * 4 + xs[dx]
-                arrived(3, slot, home_a.at[slot])
-        rows = jnp.concatenate(
-            [home_a[pl.ds(ys[dy] * 4, 4), at : at + 16, :].reshape(64, 128) for at in range(0, 64, 16)], axis=1
-        )
-        rows = jnp.concatenate([rows, rows], axis=0)
-        values = lax.dot_general(rows, back_y[...], TN, preferred_element_type=F32).astype(BF16)
-        for b in range(2):
+    def store(b, group):
+        rows = pl.ds(group * 4, 4)
+        return pltpu.make_async_copy(result.at[b, rows], out_ref.at[b, rows], store_sems.at[b, group])
+
+    for b in range(2):
+        for dy in (0, 1, 3, 2):
+            for dx in range(4):
+                if b == 0 and (dx or dy):
+                    slot = ys[dy] * 4 + xs[dx]
+                    arrived(3, slot, home_a.at[slot])
+            rows = jnp.concatenate(
+                [
+                    home_a[pl.ds(ys[dy] * 4, 4), at : at + 16, :].reshape(64, 128)
+                    for at in (b * 32, b * 32 + 16)
+                ],
+                axis=1,
+            )
+            rows = jnp.concatenate([rows, rows], axis=0)
+            values = lax.dot_general(rows, back_y[...], TN, preferred_element_type=F32).astype(BF16)
             for half in range(2):
                 for part in range(2):
                     at = pl.multiple_of((part * 8 + half * 4 + ys[dy]) * 16, 16)
                     for group in range(8):
-                        row = (b * 2 + half) * 128 + group * 16
+                        row = half * 128 + group * 16
                         lines[b, group, pl.ds(at, 16), :] = values[
                             row : row + 16, part * NY : (part + 1) * NY
                         ]
-
-    def store(b, group):
-        rows = pl.ds(group * 4, 4)
-        return pltpu.make_async_copy(result.at[b, rows], out_ref.at[b, rows], store_sems.at[b, group])
-
-    def finish(group, carry):
-        for b in range(2):
+        for group in range(8):
             values = jnp.dot(back_x[...], lines[b, group], preferred_element_type=F32)
-            rows = pl.ds(group * 4, 4)
-            total = values[:256] + values[256:] + direct[b, rows].reshape(256, NY)
+            channels = slice(group * 4, group * 4 + 4)
+            total = values[:256] + values[256:] + direct[b, channels].reshape(256, NY)
             total = 0.5 * total * (1.0 + lax.erf(total * (1.0 / math.sqrt(2.0))))
-            result[b, rows] = total.astype(BF16).reshape(4, 64, NY)
+            result[b, channels] = total.astype(BF16).reshape(4, 64, NY)
             store(b, group).start()
-        return carry
-
-    lax.fori_loop(0, 8, finish, 0)
     for copy in sent:
         copy.wait_send()
 
@@ -358,12 +364,30 @@
     lax.fori_loop(0, 8, stored, 0)
 
 
+def hand_over_kernel(source_ref, out_ref, held, load_sems, store_sems):
+    def load(part):
+        at = (part // 4, pl.ds(part % 4 * 8, 8))
+        return pltpu.make_async_copy(source_ref.at[at], held.at[at], load_sems.at[part])
+
+    def store(part):
+        at = (part // 4, pl.ds(part % 4 * 8, 8))
+        return pltpu.make_async_copy(held.at[at], out_ref.at[at], store_sems.at[part])
+
+    for part in range(8):
+        load(part).start()
+    for part in range(8):
+        load(part).wait()
+        store(part).start()
+    for part in range(8):
+        store(part).wait()
+
+
 VMEM = pl.BlockSpec(memory_space=pltpu.VMEM)
 HBM = pl.BlockSpec(memory_space=pltpu.HBM)
 
 
 def shards(field, spectral_weight, bypass_weight, bypass_bias):
-    return pl.pallas_call(
+    result = pl.pallas_call(
         exchange_kernel,
         out_shape=jax.ShapeDtypeStruct(field.shape, BF16),
         in_specs=[HBM] * 12 + [VMEM] * 2,
@@ -411,6 +435,20 @@
         bypass_weight, bypass_bias.reshape(1, 32),
     )
 
+    return pl.pallas_call(
+        hand_over_kernel,
+        out_shape=jax.ShapeDtypeStruct(field.shape, BF16),
+        in_specs=[HBM],
+        out_specs=HBM,
+        scratch_shapes=[
+            pltpu.VMEM((2, 32, 64, NY), BF16),
+            pltpu.SemaphoreType.DMA((8,)),
+            pltpu.SemaphoreType.DMA((8,)),
+        ],
+        compiler_params=pltpu.CompilerParams(vmem_limit_bytes=60 << 20),
+        name="hand_over",
+    )(result)
+
 
 def solution(mesh):
     in_specs = (P("gz", None, "gx", None), P(("gz", "gx"), None, None, None), P(), P())

time: 41.6 us -> 39.9 us (0.959)
  local copies, waits for them, and re-layouts: 3.16 us -> 0 us
  Pallas kernels: 38.2 us -> 39.7 us
    unnamed x1 -> x0, local copies, waits for them, and re-layouts: 3.16 us -> none
    pallas_call x0 -> x1, Pallas kernels: none -> 2.39 us  [shards(): pl.pallas_call(hand_over_kernel, out_shape=jax.ShapeDtypeStruct(field.sha...]
    pallas_call x1, Pallas kernels: 38.2 us -> 37.3 us  [shards(): pl.pallas_call(exchange_kernel, out_shape=jax.ShapeDtypeStruct(field.shap...]
where the time goes in v3:
time: 39.9 us; the launch traced here: 39.7 us
  Pallas kernels  39.7 us (99%)
    pallas_call x1, Pallas kernels, shards(): pl.pallas_call(exchange_kernel, out_shape=jax.ShapeDtypeStruct(field.shap...  37.3 us
    pallas_call x1, Pallas kernels, shards(): pl.pallas_call(hand_over_kernel, out_shape=jax.ShapeDtypeStruct(field.sha...  2.39 us

profile of v3, /device:TPU:1, one launch (start us, length us, event | category | flops | bytes accessed | tf_op | source)
XLA Modules:
  0.0 39.7 jit_solution(6322879654026506914)
XLA Ops:
  0.0 37.3 %exchange.1.source_ref = bf16[2,32,64,256]{3,2,1,0:T(8,128)(2,1)} custom-call(bf16[2,32,64,256]{3,2,1,0:T(8,128)(2,1)} %field_ref.1, bf16[4,2,256,256]{3,2,1,0:T(8,128)(2,1)} %constant.20.clone.table_x_ref, bf16[64,512]{1,0:T(8,128)(2,1)} %constant.21.clone.table_y_ref, bf16[4,2,32,1024]{3,2,1,0:T(8,128)(2,1)} %weight_ref.1, ...), custom_call_target="tpu_custom_call" | custom-call | tf_op jit(solution)/shard_map/exchange/pallas_call | solution.py:390
  37.3 2.4 %hand_over.1 = bf16[2,32,64,256]{3,2,1,0:T(8,128)(2,1)} custom-call(bf16[2,32,64,256]{3,2,1,0:T(8,128)(2,1)} %exchange.1.source_ref), custom_call_target="tpu_custom_call" | custom-call | tf_op jit(solution)/shard_map/hand_over/pallas_call | solution.py:438

commit v4 on v3

--- a/solution.py
+++ b/solution.py
@@ -131,7 +131,7 @@
     out_ref,
     send_a, got_a, send_b, got_b, back_b, home_b, back_a, home_a,
     field, table_x, table_y, along, weight, to_owner, channels, table_z, turn, back_z, to_grid,
-    back_y, back_x, direct_table, direct, lines, result,
+    back_y, back_x, direct_table, direct, lines_first, lines_second, result,
     sems, send_sems, recv_sems, store_sems,
 ):
     gz = lax.axis_index("gz")
@@ -260,13 +260,15 @@
 
     bypass(0)
 
-    for _, slot, _ in plane:
-        arrived(0, slot, got_a.at[slot])
     fetch_owner.wait()
     summed = jnp.zeros((256, 128), F32)
-    for sy in range(4):
+    for dy in (0, 1, 3, 2):
+        for dx in range(4):
+            if dx or dy:
+                slot = ys[dy] * 4 + xs[dx]
+                arrived(0, slot, got_a.at[slot])
         summed += jnp.dot(
-            to_owner[...], got_a[sy * 4 : sy * 4 + 4].reshape(256, 128), preferred_element_type=F32
+            to_owner[...], got_a[pl.ds(ys[dy] * 4, 4)].reshape(256, 128), preferred_element_type=F32
         )
     send_b[...] = summed.astype(BF16).reshape(16, 16, 128)
 
@@ -323,36 +325,48 @@
         rows = pl.ds(group * 4, 4)
         return pltpu.make_async_copy(result.at[b, rows], out_ref.at[b, rows], store_sems.at[b, group])
 
-    for b in range(2):
-        for dy in (0, 1, 3, 2):
-            for dx in range(4):
-                if b == 0 and (dx or dy):
-                    slot = ys[dy] * 4 + xs[dx]
-                    arrived(3, slot, home_a.at[slot])
-            rows = jnp.concatenate(
-                [
-                    home_a[pl.ds(ys[dy] * 4, 4), at : at + 16, :].reshape(64, 128)
-                    for at in (b * 32, b * 32 + 16)
-                ],
-                axis=1,
-            )
-            rows = jnp.concatenate([rows, rows], axis=0)
-            values = lax.dot_general(rows, back_y[...], TN, preferred_element_type=F32).astype(BF16)
-            for half in range(2):
-                for part in range(2):
-                    at = pl.multiple_of((part * 8 + half * 4 + ys[dy]) * 16, 16)
-                    for group in range(8):
-                        row = half * 128 + group * 16
-                        lines[b, group, pl.ds(at, 16), :] = values[
-                            row : row + 16, part * NY : (part + 1) * NY
-                        ]
-        for group in range(8):
-            values = jnp.dot(back_x[...], lines[b, group], preferred_element_type=F32)
-            channels = slice(group * 4, group * 4 + 4)
-            total = values[:256] + values[256:] + direct[b, channels].reshape(256, NY)
-            total = 0.5 * total * (1.0 + lax.erf(total * (1.0 / math.sqrt(2.0))))
-            result[b, channels] = total.astype(BF16).reshape(4, 64, NY)
-            store(b, group).start()
+    lines = (lines_first, lines_second)
+
+    def inverse_y_part(b, dy):
+        rows = jnp.concatenate(
+            [
+                home_a[pl.ds(ys[dy] * 4, 4), at : at + 16, :].reshape(64, 128)
+                for at in (b * 32, b * 32 + 16)
+            ],
+            axis=1,
+        )
+        rows = jnp.concatenate([rows, rows], axis=0)
+        values = lax.dot_general(rows, back_y[...], TN, preferred_element_type=F32).astype(BF16)
+        for half in range(2):
+            for part in range(2):
+                at = pl.multiple_of((part * 8 + half * 4 + ys[dy]) * 16, 16)
+                for group in range(8):
+                    row = half * 128 + group * 16
+                    lines[b][group, pl.ds(at, 16), :] = values[
+                        row : row + 16, part * NY : (part + 1) * NY
+                    ]
+
+    def finish(b, group):
+        values = jnp.dot(back_x[...], lines[b][group], preferred_element_type=F32)
+        channels = slice(group * 4, group * 4 + 4)
+        total = values[:256] + values[256:] + direct[b, channels].reshape(256, NY)
+        total = 0.5 * total * (1.0 + lax.erf(total * (1.0 / math.sqrt(2.0))))
+        result[b, channels] = total.astype(BF16).reshape(4, 64, NY)
+        store(b, group).start()
+
+    near = (0, 1, 3, 2)
+    for dy in near:
+        for dx in range(4):
+            if dx or dy:
+                slot = ys[dy] * 4 + xs[dx]
+                arrived(3, slot, home_a.at[slot])
+        inverse_y_part(0, dy)
+    for group in range(8):
+        if group % 2 == 0:
+            inverse_y_part(1, near[group // 2])
+        finish(0, group)
+    for group in range(8):
+        finish(1, group)
     for copy in sent:
         copy.wait_send()
 
@@ -416,7 +430,8 @@
             pltpu.VMEM((512, 256), BF16),
             pltpu.VMEM((512, 512), BF16),
             pltpu.VMEM((2, 32, 64, NY), F32),
-            pltpu.VMEM((2, 8, 256, NY), BF16),
+            pltpu.VMEM((8, 256, NY), BF16),
+            pltpu.VMEM((8, 256, NY), BF16),
             pltpu.VMEM((2, 32, 64, NY), BF16),
             pltpu.SemaphoreType.DMA((15,)),
             pltpu.SemaphoreType.DMA((4, 16)),

time: 39.9 us -> 40.1 us (level)
  no operation moved by 1% of the time
where the time goes in v4:
time: 40.1 us; the launch traced here: 39.9 us
  Pallas kernels  39.9 us (100%)
    pallas_call x1, Pallas kernels, shards(): pl.pallas_call(exchange_kernel, out_shape=jax.ShapeDtypeStruct(field.shap...  37.5 us
    pallas_call x1, Pallas kernels, shards(): pl.pallas_call(hand_over_kernel, out_shape=jax.ShapeDtypeStruct(field.sha...  2.39 us

profile of v4, /device:TPU:1, one launch (start us, length us, event | category | flops | bytes accessed | tf_op | source)
XLA Modules:
  0.0 39.9 jit_solution(10601908499112149686)
XLA Ops:
  0.0 37.5 %exchange.1.source_ref = bf16[2,32,64,256]{3,2,1,0:T(8,128)(2,1)} custom-call(bf16[2,32,64,256]{3,2,1,0:T(8,128)(2,1)} %field_ref.1, bf16[4,2,256,256]{3,2,1,0:T(8,128)(2,1)} %constant.20.clone.table_x_ref, bf16[64,512]{1,0:T(8,128)(2,1)} %constant.21.clone.table_y_ref, bf16[4,2,32,1024]{3,2,1,0:T(8,128)(2,1)} %weight_ref.1, ...), custom_call_target="tpu_custom_call" | custom-call | tf_op jit(solution)/shard_map/exchange/pallas_call | solution.py:404
  37.5 2.4 %hand_over.1 = bf16[2,32,64,256]{3,2,1,0:T(8,128)(2,1)} custom-call(bf16[2,32,64,256]{3,2,1,0:T(8,128)(2,1)} %exchange.1.source_ref), custom_call_target="tpu_custom_call" | custom-call | tf_op jit(solution)/shard_map/hand_over/pallas_call | solution.py:453
